TPU v7x, 32 devices: a whole 2x2x4 slice. The times are simulated.
32 devices in a mesh: gx: 2 (over y), gy: 4 (over z), gz: 4 (over x, core).
Axes of the slice: x: 2, y: 2, z: 4, core: 2. Of those that a mesh axis runs over, the one named last changes fastest.
Arguments:
- source: bfloat16 [8, 96, 2048], P('gx', 'gy', 'gz'), may hold values from -6 to 6
- tangent: bfloat16 [8, 96, 2048], P('gx', 'gy', 'gz'), may hold values from -6 to 6
- first_weight: bfloat16 [3, 3, 3, 64, 64], replicated, may hold values from -0.15625 to 0.15625
- first_bias: float32 [64], replicated, may hold values from -3 to 3
- second_weight: bfloat16 [3, 3, 3, 64, 64], replicated, may hold values from -0.15625 to 0.15625
- second_bias: float32 [64], replicated, may hold values from -3 to 3
Outputs:
- result: bfloat16 [8, 96, 2048], P('gx', 'gy', 'gz')
- result_tangent: bfloat16 [8, 96, 2048], P('gx', 'gy', 'gz')
All inputs are finite; a program needn't handle non-finite values.
Results may differ from a plain program's by a relative error of at most 0.0052.
Values may be sent and summed in bfloat16 or wider, within the bound.
A program may use at most 64 MiB of HBM per device.

v0:
```python
import jax
import jax.numpy as jnp
import numpy as np
from jax import lax
from jax.sharding import PartitionSpec as P


def padded_2(cells, sides, width):
    for axis, dim in sides:
        count = lax.axis_size(axis)
        ends = count - 1
        head = lax.slice_in_dim(cells, 0, width, axis=dim)
        tail = lax.slice_in_dim(cells, cells.shape[dim] - width, cells.shape[dim], axis=dim)
        cells = jnp.concatenate(
            [
                lax.ppermute(tail, axis, [(i, (i + 1) % count) for i in range(ends)]),
                cells,
                lax.ppermute(head, axis, [((i + 1) % count, i) for i in range(ends)]),
            ],
            axis=dim,
        )
    return cells


def pair_table():
    table = np.zeros((3, 2, 2, 3), np.float32)
    for shift in range(3):
        for inner in range(2):
            for outer in range(2):
                offset = 2 * (shift - 1) + inner - outer + 1
                if 0 <= offset <= 2:
                    table[shift, inner, outer, offset] = 1.0
    return table


def pair_kernels(weight):
    width = weight.shape[3]
    mats = jnp.einsum("kijz,abzco->abkicjo", jnp.asarray(pair_table()), weight.astype(jnp.float32))
    return mats.reshape(3, 3, 3, 2 * width, 2 * width).astype(jnp.bfloat16)


def convolve(padded, kernels, out_x, out_y, pairs):
    lanes = kernels.shape[3]
    view = padded.reshape(2, out_x + 2, out_y + 2, pairs + 2, lanes)
    total = jnp.zeros((2, out_x, out_y, pairs, lanes), jnp.float32)
    for ox in range(3):
        for oy in range(3):
            for oz in range(3):
                window = view[:, ox : ox + out_x, oy : oy + out_y, oz : oz + pairs, :]
                total = total + jnp.einsum(
                    "sabcl,lm->sabcm",
                    window,
                    kernels[ox, oy, oz],
                    preferred_element_type=jnp.float32,
                )
    return total


def silu_slope(pre):
    sig = jax.nn.sigmoid(pre)
    return sig * (1.0 + pre * (1.0 - sig))


def deep_width_pad(field, lanes):
    return padded_2(field, (("gz", 3),), lanes)


def inside_rows(position, devices, block, count):
    rows = position * block - 1 + jnp.arange(count, dtype=jnp.int32)
    return (rows >= 0) & (rows < block * devices)


def shards(source, tangent, first_weight, first_bias, second_weight, second_bias):
    depth, height, flat = source.shape
    width = first_weight.shape[3]
    lanes = 2 * width
    pairs = flat // lanes
    kernels_one = pair_kernels(first_weight)
    kernels_two = pair_kernels(second_weight)
    bias_one = jnp.concatenate([first_bias, first_bias])
    bias_two = jnp.concatenate([second_bias, second_bias])
    stacked = jnp.stack([source, tangent])
    extended = padded_2(stacked, (("gx", 1), ("gy", 2)), 2)
    out_x, out_y = (depth + 2, height + 2)
    first = convolve(deep_width_pad(extended, lanes), kernels_one, out_x, out_y, pairs)
    inside_x = inside_rows(lax.axis_index("gx"), lax.axis_size("gx"), depth, out_x)
    inside_y = inside_rows(lax.axis_index("gy"), lax.axis_size("gy"), height, out_y)
    inside = (inside_x[:, None] & inside_y[None, :]).astype(jnp.float32)[:, :, None, None]
    pre_one = first[0] + bias_one
    hidden = (jax.nn.silu(pre_one) * inside).astype(jnp.bfloat16)
    hidden_tangent = (silu_slope(pre_one) * first[1] * inside).astype(jnp.bfloat16)
    layer = jnp.stack([hidden, hidden_tangent]).reshape(2, out_x, out_y, flat)
    padded_two = deep_width_pad(layer, lanes)
    second = convolve(padded_two, kernels_two, depth, height, pairs)
    pre_two = second[0] + bias_two
    result = jax.nn.silu(pre_two).astype(jnp.bfloat16).reshape(depth, height, flat)
    result_tangent = (
        (silu_slope(pre_two) * second[1]).astype(jnp.bfloat16).reshape(depth, height, flat)
    )
    return (result, result_tangent)


def solution(mesh):
    return jax.shard_map(
        shards,
        mesh=mesh,
        in_specs=(P("gx", "gy", "gz"), P("gx", "gy", "gz"), P(), P(), P(), P()),
        out_specs=(P("gx", "gy", "gz"), P("gx", "gy", "gz")),
        check_vma=False,
    )
```

profile of v0, /device:TPU:1, one launch (start us, length us, event | category | flops | bytes accessed | tf_op | source)
XLA Modules:
  0.0 73.6 jit_solution(970663981782850229)
XLA Ops:
  0.6 1.1 %copy_bitcast_fusion = (bf16[1,4,24,512]{3,1,2,0:T(4,128)(2,1)S(1)}, bf16[1,4,24,512]{3,1,2,0:T(4,128)(2,1)S(1)}) fusion(bf16[4,24,512]{2,1,0:T(8,128)(2,1)} %param.9, bf16[4,24,512]{2,1,0:T(8,128)(2,1)} %param.8), kind=kLoop, calls=%fused_computation.133 | loop fusion | bytes 393216 | tf_op jit(solution)/shard_map/stack | solution.py:82
  1.9 4.0 %collective-permute-start = (bf16[2,2,24,512]{3,1,2,0:T(2,128)(2,1)S(1)}, bf16[2,2,24,512]{3,1,2,0:T(2,128)(2,1)S(1)}, u32[]{:S(2)}, u32[]{:S(2)}) collective-permute-start(bf16[2,2,24,512]{3,1,2,0:T(2,128)(2,1)S(1)} %get-tuple-element.68), channel_id=1, source_target_pairs={{0,16},{1,17},{2,18},{3,19},{4,20},{5,21},{6,22},{7,23},{8,24},{9,... | collective-permute-start | bytes 294920 | tf_op jit(solution)/shard_map/ppermute | solution.py:16
  5.9 1.3 %collective-permute-start.1 = (bf16[2,2,24,512]{3,1,2,0:T(2,128)(2,1)S(1)}, bf16[2,2,24,512]{3,1,2,0:T(2,128)(2,1)S(1)}, u32[]{:S(2)}, u32[]{:S(2)}) collective-permute-start(bf16[2,2,24,512]{3,1,2,0:T(2,128)(2,1)S(1)} %get-tuple-element.69), channel_id=1, source_target_pairs={{16,0},{17,1},{18,2},{19,3},{20,4},{21,5},{22,6},{23,7},{24,8},{25... | collective-permute-start | bytes 294920 | tf_op jit(solution)/shard_map/ppermute | solution.py:18
  7.3 1.9 %convert_bitcast_fusion.1 = bf16[3,3,3,2,64,2,64]{6,2,4,1,0,5,3:T(4,128)(2,1)S(1)} fusion(bf16[3,2,2,3,1,1,1]{3,0,6,5,4,2,1:T(4,128)(2,1)} %constant.75, bf16[3,3,3,64,64,1,1]{4,3,2,1,0,6,5:T(8,128)(2,1)S(1)} %bitcast.397), kind=kOutput, calls=%fused_computation.1 | convolution fusion | flops 2654208 | bytes 1105992 | tf_op jit(solution)/shard_map/kijz,abzco->abkicjo/dot_general | solution.py:38
  9.2 1.2 %convert_bitcast_fusion = bf16[3,3,3,2,64,2,64]{6,2,4,1,0,5,3:T(4,128)(2,1)S(1)} fusion(bf16[3,2,2,3,1,1,1]{3,0,6,5,4,2,1:T(4,128)(2,1)S(1)} %copy-done.3, bf16[3,3,3,64,64,1,1]{4,3,2,1,0,6,5:T(8,128)(2,1)S(1)} %bitcast.398), kind=kOutput, calls=%fused_computation | convolution fusion | flops 2654208 | bytes 1105992 | tf_op jit(solution)/shard_map/kijz,abzco->abkicjo/dot_general | solution.py:38
  10.4 0.9 %collective-permute-done.1 = bf16[2,2,24,512]{3,1,2,0:T(2,128)(2,1)S(1)} collective-permute-done((bf16[2,2,24,512]{3,1,2,0:T(2,128)(2,1)S(1)}, bf16[2,2,24,512]{3,1,2,0:T(2,128)(2,1)S(1)}, u32[]{:S(2)}, u32[]{:S(2)}) %collective-permute-start.1) | collective-permute-done | bytes 98336 | tf_op jit(solution)/shard_map/ppermute | solution.py:18
  11.3 3.2 %collective-permute-start.2 = (bf16[2,8,2,512]{3,1,2,0:T(8,128)(2,1)S(1)}, bf16[2,8,2,512]{3,1,2,0:T(8,128)(2,1)S(1)}, u32[]{:S(2)}, u32[]{:S(2)}) collective-permute-start(bf16[2,8,2,512]{3,1,2,0:T(8,128)(2,1)S(1)} %get-tuple-element.64), channel_id=1, source_target_pairs={{0,4},{4,8},{8,12},{1,5},{5,9},{9,13},{2,6},{6,10},{10,14},{3,7},{... | collective-permute-start | bytes 98312 | tf_op jit(solution)/shard_map/ppermute | solution.py:16
  14.5 1.3 %collective-permute-start.3 = (bf16[2,8,2,512]{3,1,2,0:T(8,128)(2,1)S(1)}, bf16[2,8,2,512]{3,1,2,0:T(8,128)(2,1)S(1)}, u32[]{:S(2)}, u32[]{:S(2)}) collective-permute-start(bf16[2,8,2,512]{3,1,2,0:T(8,128)(2,1)S(1)} %get-tuple-element.65), channel_id=1, source_target_pairs={{4,0},{8,4},{12,8},{5,1},{9,5},{13,9},{6,2},{10,6},{14,10},{7,3},{... | collective-permute-start | bytes 98312 | tf_op jit(solution)/shard_map/ppermute | solution.py:18
  15.9 3.3 %collective-permute-done.3 = bf16[2,8,2,512]{3,1,2,0:T(8,128)(2,1)S(1)} collective-permute-done((bf16[2,8,2,512]{3,1,2,0:T(8,128)(2,1)S(1)}, bf16[2,8,2,512]{3,1,2,0:T(8,128)(2,1)S(1)}, u32[]{:S(2)}, u32[]{:S(2)}) %collective-permute-start.3) | collective-permute-done | bytes 32800 | tf_op jit(solution)/shard_map/ppermute | solution.py:18
  19.2 0.9 %pad_maximum_fusion.6 = (bf16[2,8,28,128]{3,1,2,0:T(8,128)(2,1)}, bf16[2,8,28,128]{3,1,2,0:T(8,128)(2,1)}) fusion(bf16[2,8,2,512]{3,1,2,0:T(8,128)(2,1)S(1)} %collective-permute-done.3, bf16[2,8,2,512]{3,1,2,0:T(8,128)(2,1)S(1)} %collective-permute-done.2, bf16[2,2,24,512]{3,1,2,0:T(2,128)(2,1)S(1)} %collective-permute-done.1, ...), kind=kLoop, calls=%fused_computation.130 | loop fusion | flops 1376256 | bytes 688128 | tf_op jit(solution)/shard_map/slice | solution.py:13
  20.1 6.5 %collective-permute-start.4 = (bf16[2,8,28,128]{3,1,2,0:T(8,128)(2,1)}, bf16[2,8,28,128]{3,1,2,0:T(8,128)(2,1)S(1)}, u32[]{:S(2)}, u32[]{:S(2)}) collective-permute-start(bf16[2,8,28,128]{3,1,2,0:T(8,128)(2,1)} %get-tuple-element.58), channel_id=1, source_target_pairs={{0,1},{1,2},{2,3},{4,5},{5,6},{6,7},{8,9},{9,10},{10,11},{12,13},{... | collective-permute-start | bytes 344072 | tf_op jit(solution)/shard_map/ppermute | solution.py:16
  26.6 1.9 %collective-permute-start.5 = (bf16[2,8,28,128]{3,1,2,0:T(8,128)(2,1)}, bf16[2,8,28,128]{3,1,2,0:T(8,128)(2,1)S(1)}, u32[]{:S(2)}, u32[]{:S(2)}) collective-permute-start(bf16[2,8,28,128]{3,1,2,0:T(8,128)(2,1)} %get-tuple-element.59), channel_id=1, source_target_pairs={{1,0},{2,1},{3,2},{5,4},{6,5},{7,6},{9,8},{10,9},{11,10},{13,12},{... | collective-permute-start | bytes 344072 | tf_op jit(solution)/shard_map/ppermute | solution.py:18
  28.6 3.4 %copy.16 = bf16[3,3,3,2,64,2,64]{6,5,4,3,2,1,0:T(2,128)(2,1)} copy(bf16[3,3,3,2,64,2,64]{6,2,4,1,0,5,3:T(4,128)(2,1)S(1)} %convert_bitcast_fusion.1) | data formatting | bytes 1769472 | tf_op jit(solution)/shard_map/convert_element_type | solution.py:39
  32.0 4.2 %convert_element_type.45 = bf16[3,3,3,128,128]{4,3,2,1,0:T(8,128)(2,1)} reshape(bf16[3,3,3,2,64,2,64]{6,5,4,3,2,1,0:T(2,128)(2,1)} %copy.16) | data formatting | bytes 1769472 | tf_op jit(solution)/shard_map/convert_element_type | solution.py:39
  36.3 0.4 maximum_bitcast_fusion
  36.7 0.6 fusion.62
  37.3 2.4 %fusion.61 = (bf16[2,6,26,4,128]{4,1,3,2,0:T(8,128)(2,1)S(1)}, bf16[2,6,26,4,128]{4,1,3,2,0:T(8,128)(2,1)S(1)}, bf16[2,6,26,4,128]{4,1,3,2,0:T(8,128)(2,1)S(1)},...) fusion(bf16[2,8,28,6,128]{4,1,3,2,0:T(8,128)(2,1)S(1)} %maximum, ...), kind=kLoop, calls=%fused_computation.201 | loop fusion | bytes 12140544 | tf_op jit(solution)/shard_map/slice | solution.py:49
  39.7 0.3 fusion.30
  40.0 0.3 convolution_add_fusion.25
  40.3 0.3 convolution_add_fusion.24
  40.5 0.3 convolution_add_fusion.23
  40.8 0.3 convolution_add_fusion.22
  41.1 0.3 convolution_add_fusion.21
  41.4 0.3 convolution_add_fusion.20
  41.6 0.3 convolution_add_fusion.19
  41.9 0.3 convolution_add_fusion.18
  42.2 0.3 convolution_add_fusion.17
  42.5 0.3 convolution_add_fusion.16
  42.7 0.3 convolution_add_fusion.15
  43.0 0.3 convolution_add_fusion.14
  43.3 0.3 convolution_add_fusion.13
  43.6 0.3 convolution_add_fusion.12
  43.8 0.3 convolution_add_fusion.11
  44.1 0.3 convolution_add_fusion.10
  44.4 0.3 convolution_add_fusion.9
  44.7 0.3 convolution_add_fusion.8
  44.9 0.3 convolution_add_fusion.7
  45.2 0.3 convolution_add_fusion.6
  45.5 0.3 convolution_add_fusion.5
  45.8 0.3 convolution_add_fusion.4
  46.0 0.3 convolution_add_fusion.3
  46.3 0.3 convolution_add_fusion.2
  46.6 0.3 convolution_add_fusion.1
  46.9 0.3 convolution_add_fusion
  47.1 0.9 %fusion.3 = (bf16[1,6,26,4,128]{4,2,3,1,0:T(8,128)(2,1)}, bf16[1,6,26,4,128]{4,2,3,1,0:T(8,128)(2,1)S(1)}) fusion(f32[2,6,26,4,128]{4,2,3,1,0:T(8,128)S(1)} %convolution_add_fusion, f32[6,26]{1,0:T(8,128)S(1)} %and_convert_fusion, f32[128]{0:T(128)S(1)} %pad_maximum_fusion.12), kind=kLoop, calls=%fused_computation.60 | loop fusion | flops 1118208 | bytes 959600 | tf_op jit(solution)/shard_map/convert_element_type | solution.py:91
  48.2 1.0 %copy.44 = bf16[1,6,26,4,128]{4,3,2,1,0:T(4,128)(2,1)S(1)} copy(bf16[1,6,26,4,128]{4,2,3,1,0:T(8,128)(2,1)} %get-tuple-element.2) | data formatting | bytes 319488 | tf_op jit(solution)/shard_map/convert_element_type | solution.py:91
  49.3 0.7 fusion.66
  50.0 3.6 %collective-permute-start.6 = (bf16[2,6,26,128]{3,2,1,0:T(8,128)(2,1)}, bf16[2,6,26,128]{3,2,1,0:T(8,128)(2,1)S(1)}, u32[]{:S(2)}, u32[]{:S(2)}) collective-permute-start(bf16[2,6,26,128]{3,2,1,0:T(8,128)(2,1)} %get-tuple-element.62), channel_id=1, source_target_pairs={{0,1},{1,2},{2,3},{4,5},{5,6},{6,7},{8,9},{9,10},{10,11},{12,13},{... | collective-permute-start | bytes 239624 | tf_op jit(solution)/shard_map/ppermute | solution.py:16
  53.7 2.1 %collective-permute-start.7 = (bf16[2,6,26,128]{3,2,1,0:T(8,128)(2,1)S(1)}, bf16[2,6,26,128]{3,2,1,0:T(8,128)(2,1)S(1)}, u32[]{:S(2)}, u32[]{:S(2)}) collective-permute-start(bf16[2,6,26,128]{3,2,1,0:T(8,128)(2,1)S(1)} %get-tuple-element.63), channel_id=1, source_target_pairs={{1,0},{2,1},{3,2},{5,4},{6,5},{7,6},{9,8},{10,9},{11,10},{13,12},{... | collective-permute-start | bytes 239624 | tf_op jit(solution)/shard_map/ppermute | solution.py:18
  55.8 3.4 %copy.48 = bf16[3,3,3,2,64,2,64]{6,5,4,3,2,1,0:T(2,128)(2,1)} copy(bf16[3,3,3,2,64,2,64]{6,2,4,1,0,5,3:T(4,128)(2,1)S(1)} %convert_bitcast_fusion) | data formatting | bytes 1769472 | tf_op jit(solution)/shard_map/convert_element_type | solution.py:39
  59.2 3.4 %convert_element_type.51 = bf16[3,3,3,128,128]{4,3,2,1,0:T(8,128)(2,1)S(1)} reshape(bf16[3,3,3,2,64,2,64]{6,5,4,3,2,1,0:T(2,128)(2,1)} %copy.48) | data formatting | bytes 1769472 | tf_op jit(solution)/shard_map/convert_element_type | solution.py:39
  62.7 0.6 reshape.127
  63.3 0.6 fusion.64
  63.9 1.7 %fusion.63 = (bf16[2,4,24,4,128]{4,3,2,1,0:T(4,128)(2,1)S(1)}, bf16[2,4,24,4,128]{4,3,2,1,0:T(4,128)(2,1)S(1)}, bf16[2,4,24,4,128]{4,3,2,1,0:T(4,128)(2,1)S(1)},...) fusion(bf16[2,6,26,6,128]{4,3,2,1,0:T(8,128)(2,1)S(1)} %reshape.127), kind=kLoop, calls=%fused_computation.203 | loop fusion | bytes 7471104 | tf_op jit(solution)/shard_map/slice | solution.py:49
  65.9 0.3 convolution_add_fusion.51
  66.9 0.3 convolution_add_fusion.47
  67.7 0.3 convolution_add_fusion.44
  68.5 0.3 convolution_add_fusion.41
  68.7 0.3 convolution_add_fusion.40
  69.5 0.3 convolution_add_fusion.37
  70.5 0.3 convolution_add_fusion.33
  71.2 0.3 convolution_add_fusion.30
  72.3 0.3 convolution_add_fusion.26
  72.9 0.8 %multiply_convert_fusion.1 = (bf16[4,24,512]{2,1,0:T(8,128)(2,1)}, bf16[4,24,512]{2,1,0:T(8,128)(2,1)}) fusion(f32[4,24,512]{2,1,0:T(8,128)S(1)} %squeeze.225, f32[4,24,512]{2,1,0:T(8,128)S(1)} %squeeze.224, f32[512]{0:T(512)S(1)} %broadcast_bitcast_fusion), kind=kLoop, calls=%fused_computation.122 | loop fusion | flops 589824 | bytes 591872 | tf_op jit(solution)/shard_map/convert_element_type | solution.py:98
  (55 shorter events, 5.5 us)
Async XLA Ops:
  0.6 6.6 %copy-start = (bf16[3,3,3,64,64]{4,3,2,1,0:T(8,128)(2,1)S(1)}, bf16[3,3,3,64,64]{4,3,2,1,0:T(8,128)(2,1)}, u32[]{:S(2)}) copy-start(bf16[3,3,3,64,64]{4,3,2,1,0:T(8,128)(2,1)} %param.10) | copy-start | bytes 663556
  1.9 8.5 %collective-permute-start = (bf16[2,2,24,512]{3,1,2,0:T(2,128)(2,1)S(1)}, bf16[2,2,24,512]{3,1,2,0:T(2,128)(2,1)S(1)}, u32[]{:S(2)}, u32[]{:S(2)}) collective-permute-start(bf16[2,2,24,512]{3,1,2,0:T(2,128)(2,1)S(1)} %get-tuple-element.68), channel_id=1, source_target_pairs={{0,16},{1,17},{2,18},{3,19},{4,20},{5,21},{6,22},{7,23},{8,24},{9,... | collective-permute-start | bytes 294920 | tf_op jit(solution)/shard_map/ppermute | solution.py:16
  5.9 5.4 %collective-permute-start.1 = (bf16[2,2,24,512]{3,1,2,0:T(2,128)(2,1)S(1)}, bf16[2,2,24,512]{3,1,2,0:T(2,128)(2,1)S(1)}, u32[]{:S(2)}, u32[]{:S(2)}) collective-permute-start(bf16[2,2,24,512]{3,1,2,0:T(2,128)(2,1)S(1)} %get-tuple-element.69), channel_id=1, source_target_pairs={{16,0},{17,1},{18,2},{19,3},{20,4},{21,5},{22,6},{23,7},{24,8},{25... | collective-permute-start | bytes 294920 | tf_op jit(solution)/shard_map/ppermute | solution.py:18
  7.2 1.9 %copy-start.2 = (bf16[3,3,3,64,64]{4,3,2,1,0:T(8,128)(2,1)S(1)}, bf16[3,3,3,64,64]{4,3,2,1,0:T(8,128)(2,1)}, u32[]{:S(2)}) copy-start(bf16[3,3,3,64,64]{4,3,2,1,0:T(8,128)(2,1)} %param.12) | copy-start | bytes 663556
  7.2 1.9 %copy-start.3 = (bf16[3,2,2,3,1,1,1]{3,0,6,5,4,2,1:T(4,128)(2,1)S(1)}, bf16[3,2,2,3,1,1,1]{3,0,6,5,4,2,1:T(4,128)(2,1)}, u32[]{:S(2)}) copy-start(bf16[3,2,2,3,1,1,1]{3,0,6,5,4,2,1:T(4,128)(2,1)} %constant.75) | copy-start | bytes 220
  9.2 19.3 %copy-start.4 = (f32[64]{0:T(128)S(1)}, f32[64]{0:T(128)}, u32[]{:S(2)}) copy-start(f32[64]{0:T(128)} %param.11) | copy-start | bytes 772
  11.3 4.6 %collective-permute-start.2 = (bf16[2,8,2,512]{3,1,2,0:T(8,128)(2,1)S(1)}, bf16[2,8,2,512]{3,1,2,0:T(8,128)(2,1)S(1)}, u32[]{:S(2)}, u32[]{:S(2)}) collective-permute-start(bf16[2,8,2,512]{3,1,2,0:T(8,128)(2,1)S(1)} %get-tuple-element.64), channel_id=1, source_target_pairs={{0,4},{4,8},{8,12},{1,5},{5,9},{9,13},{2,6},{6,10},{10,14},{3,7},{... | collective-permute-start | bytes 98312 | tf_op jit(solution)/shard_map/ppermute | solution.py:16
  14.5 4.7 %collective-permute-start.3 = (bf16[2,8,2,512]{3,1,2,0:T(8,128)(2,1)S(1)}, bf16[2,8,2,512]{3,1,2,0:T(8,128)(2,1)S(1)}, u32[]{:S(2)}, u32[]{:S(2)}) collective-permute-start(bf16[2,8,2,512]{3,1,2,0:T(8,128)(2,1)S(1)} %get-tuple-element.65), channel_id=1, source_target_pairs={{4,0},{8,4},{12,8},{5,1},{9,5},{13,9},{6,2},{10,6},{14,10},{7,3},{... | collective-permute-start | bytes 98312 | tf_op jit(solution)/shard_map/ppermute | solution.py:18
  20.1 16.2 %collective-permute-start.4 = (bf16[2,8,28,128]{3,1,2,0:T(8,128)(2,1)}, bf16[2,8,28,128]{3,1,2,0:T(8,128)(2,1)S(1)}, u32[]{:S(2)}, u32[]{:S(2)}) collective-permute-start(bf16[2,8,28,128]{3,1,2,0:T(8,128)(2,1)} %get-tuple-element.58), channel_id=1, source_target_pairs={{0,1},{1,2},{2,3},{4,5},{5,6},{6,7},{8,9},{9,10},{10,11},{12,13},{... | collective-permute-start | bytes 344072 | tf_op jit(solution)/shard_map/ppermute | solution.py:16
  26.6 9.7 %collective-permute-start.5 = (bf16[2,8,28,128]{3,1,2,0:T(8,128)(2,1)}, bf16[2,8,28,128]{3,1,2,0:T(8,128)(2,1)S(1)}, u32[]{:S(2)}, u32[]{:S(2)}) collective-permute-start(bf16[2,8,28,128]{3,1,2,0:T(8,128)(2,1)} %get-tuple-element.59), channel_id=1, source_target_pairs={{1,0},{2,1},{3,2},{5,4},{6,5},{7,6},{9,8},{10,9},{11,10},{13,12},{... | collective-permute-start | bytes 344072 | tf_op jit(solution)/shard_map/ppermute | solution.py:18
  32.0 4.2 %copy-start.5 = (f32[64]{0:T(128)S(1)}, f32[64]{0:T(128)}, u32[]{:S(2)}) copy-start(f32[64]{0:T(128)} %param.13) | copy-start | bytes 772
  37.3 2.4 %copy-start.1 = (bf16[3,3,3,128,128]{4,3,2,1,0:T(8,128)(2,1)S(1)}, bf16[3,3,3,128,128]{4,3,2,1,0:T(8,128)(2,1)}, u32[]{:S(2)}) copy-start(bf16[3,3,3,128,128]{4,3,2,1,0:T(8,128)(2,1)} %convert_element_type.45) | copy-start | bytes 2654212
  50.0 12.6 %collective-permute-start.6 = (bf16[2,6,26,128]{3,2,1,0:T(8,128)(2,1)}, bf16[2,6,26,128]{3,2,1,0:T(8,128)(2,1)S(1)}, u32[]{:S(2)}, u32[]{:S(2)}) collective-permute-start(bf16[2,6,26,128]{3,2,1,0:T(8,128)(2,1)} %get-tuple-element.62), channel_id=1, source_target_pairs={{0,1},{1,2},{2,3},{4,5},{5,6},{6,7},{8,9},{9,10},{10,11},{12,13},{... | collective-permute-start | bytes 239624 | tf_op jit(solution)/shard_map/ppermute | solution.py:16
  53.7 9.0 %collective-permute-start.7 = (bf16[2,6,26,128]{3,2,1,0:T(8,128)(2,1)S(1)}, bf16[2,6,26,128]{3,2,1,0:T(8,128)(2,1)S(1)}, u32[]{:S(2)}, u32[]{:S(2)}) collective-permute-start(bf16[2,6,26,128]{3,2,1,0:T(8,128)(2,1)S(1)} %get-tuple-element.63), channel_id=1, source_target_pairs={{1,0},{2,1},{3,2},{5,4},{6,5},{7,6},{9,8},{10,9},{11,10},{13,12},{... | collective-permute-start | bytes 239624 | tf_op jit(solution)/shard_map/ppermute | solution.py:18
where the time goes:
time: 74.1 us; the launch traced here: 73.6 us
  starting transfers between devices  24 us (32%)
  local copies, waits for them, and re-layouts  23.7 us (32%)
  matrix products  17 us (23%)
  waiting for transfers between devices  4.17 us (6%)
  other arithmetic  3.44 us (5%)
  between operations  1.38 us (2%)
    ppermute x4, starting transfers between devices, padded_2(): lax.ppermute(tail, axis, [(i, (i + 1) % count) for i in range(ends)])  17.3 us
    convert_element_type x4, local copies, waits for them, and re-layouts, pair_kernels(): return mats.reshape(3, 3, 3, 2 * width, 2 * width).astype(jnp.bfloat16)  14.4 us
    dot_general x54, matrix products, convolve(): jnp.einsum('sabcl,lm->sabcm', window, kernels[ox, oy, oz], preferred_elem...  13.9 us
    ppermute x4, starting transfers between devices, padded_2(): lax.ppermute(head, axis, [((i + 1) % count, i) for i in range(ends)])  6.65 us
    slice x4, local copies, waits for them, and re-layouts, convolve(): window = view[:, ox:ox + out_x, oy:oy + out_y, oz:oz + pairs, :]  5.35 us
    ppermute x4, waiting for transfers between devices, padded_2(): lax.ppermute(head, axis, [((i + 1) % count, i) for i in range(ends)])  4.16 us
    dot_general x2, matrix products, pair_kernels(): jnp.einsum('kijz,abzco->abkicjo', jnp.asarray(pair_table()), weight.astyp...  3.05 us
  transfers between devices with their start and end apart: 8, of which 2 were waited for; matrix products, arithmetic and copies ran while one was open for 24% of the time, Pallas kernels for 0%

commit v1 on v0

v1 whole, which is shorter than its diff:
```python
import functools

import jax
import jax.numpy as jnp
from jax import lax
from jax.experimental import pallas as pl
from jax.experimental.pallas import tpu as pltpu
from jax.sharding import PartitionSpec as P

MESH = pl.DeviceIdType.MESH
F32 = jnp.float32
BF16 = jnp.bfloat16
ROWS = 32
PLANE = [(dy, dz) for dy in (-1, 0, 1) for dz in (-1, 0, 1) if dy or dz]
X_MSG = {(s, f): 2 * s + f for s in range(2) for f in range(2)}
A_Z = {(s, f): 4 + 2 * s + f for s in range(2) for f in range(2)}
A_S = {(s, z): 8 + 3 * s + z for s in range(2) for z in range(3)}
B_Z = {(s, k): 14 + 2 * s + k for s in range(2) for k in range(2)}
B_S = {(s, z): 18 + 3 * s + z for s in range(2) for z in range(3)}
MESSAGES = 24
STEP = (-1, 1)


def band_store(band, weight):
    zero64 = jnp.zeros((64, 64), BF16)
    zero128 = jnp.zeros((128, 128), BF16)
    for dx in range(3):
        for dy in range(3):
            taps = weight[dx, dy].reshape(192, 64)
            pair = jnp.concatenate(
                [
                    jnp.concatenate([taps, zero64], axis=0),
                    jnp.concatenate([zero64, taps], axis=0),
                ],
                axis=1,
            )
            r, c = dx * 384, dy * 256
            band[r : r + 256, c : c + 128] = pair
            band[r + 256 : r + 384, c : c + 128] = zero128
            band[r : r + 128, c + 128 : c + 256] = zero128
            band[r + 128 : r + 384, c + 128 : c + 256] = pair


def pack_strips(field, strips):
    row = lax.broadcasted_iota(jnp.int32, (8, 512), 0)
    low, high = [], []
    for f in range(2):
        first = jnp.zeros((8, 512), F32)
        last = jnp.zeros((8, 512), F32)
        for x in range(4):
            here = (row // 2) == x
            top = field[f, x, 0:8, :].astype(F32)
            end = field[f, x, 16:24, :].astype(F32)
            if x:
                top = pltpu.roll(top, 2 * x, 0)
            if x != 3:
                end = pltpu.roll(end, 2 + 2 * x, 0)
            first = jnp.where(here, top, first)
            last = jnp.where(here, end, last)
        low.append(first)
        high.append(last)
    strips[0] = jnp.concatenate(low, axis=0).astype(BF16)
    strips[1] = jnp.concatenate(high, axis=0).astype(BF16)


def assemble(grid, places, field, z_halo, strips):
    row = lax.broadcasted_iota(jnp.int32, (8, 768), 0)
    for f in range(2):
        above = strips[1].astype(F32)[8 * f : 8 * f + 8]
        below = strips[0].astype(F32)[8 * f : 8 * f + 8]
        for x in range(4):
            place = places[x]
            grid[f, place, 0:24, 0:128] = z_halo[1, f, x]
            grid[f, place, 0:24, 128:640] = field[f, x]
            grid[f, place, 0:24, 640:768] = z_halo[0, f, x]
            down = pltpu.roll(below, (8 - 2 * x) % 8, 0) if x else below
            up = pltpu.roll(above, 6 - 2 * x, 0) if x != 3 else above
            edge = jnp.where(row < 2, down, jnp.where(row >= 6, up, 0.0))
            grid[f, place, 24:32, :] = edge.astype(BF16)


def taps_sum(part, count, lanes):
    part = part.reshape(2 * count, ROWS, 3 * lanes)
    return (
        pltpu.roll(part[:, :, 0:lanes], 1, 1)
        + part[:, :, lanes : 2 * lanes]
        + pltpu.roll(part[:, :, 2 * lanes : 3 * lanes], ROWS - 1, 1)
    ).reshape(2, count, ROWS, lanes)


def conv_wide(grid, band, first, count, lane):
    rows = [
        grid[:, first + dx : first + dx + count, :, lane : lane + 384].reshape(
            2 * count * ROWS, 384
        )
        for dx in range(3)
    ]
    part = jnp.dot(
        jnp.concatenate(rows, axis=1), band[...], preferred_element_type=F32
    )
    return taps_sum(part, count, 256)


def conv_narrow(grid, band, first, count, lane):
    rows = [
        grid[:, first + dx : first + dx + count, :, lane : lane + 256].reshape(
            2 * count * ROWS, 256
        )
        for dx in range(3)
    ]
    weights = jnp.concatenate(
        [
            jnp.concatenate(
                [band[dx * 384 : dx * 384 + 256, dy * 256 : dy * 256 + 128] for dy in range(3)],
                axis=1,
            )
            for dx in range(3)
        ],
        axis=0,
    )
    part = jnp.dot(jnp.concatenate(rows, axis=1), weights, preferred_element_type=F32)
    return taps_sum(part, count, 128)


def silu_pair(total, bias):
    pre = total[0] + bias
    sig = jax.nn.sigmoid(pre)
    return pre * sig, sig * (1.0 + pre * (1.0 - sig)) * total[1]


def kernel(
    nx,
    ny,
    nz,
    source,
    tangent,
    w_one,
    b_one,
    w_two,
    b_two,
    out,
    out_tangent,
    own,
    x_halo,
    z_halo,
    strip_send,
    strip_halo,
    weights,
    bands,
    grid,
    hidden,
    local_sem,
    send_sem,
    recv_sem,
):
    ix, iy, iz = lax.axis_index("gx"), lax.axis_index("gy"), lax.axis_index("gz")

    def has(dx, dy, dz):
        ok = None
        for i, n, d in ((ix, nx, dx), (iy, ny, dy), (iz, nz, dz)):
            if d:
                this = (i > 0) if d < 0 else (i < n - 1)
                ok = this if ok is None else ok & this
        return ok

    inputs = (source, tangent)
    loads = [
        pltpu.make_async_copy(source, own.at[0], local_sem.at[0]),
        pltpu.make_async_copy(tangent, own.at[1], local_sem.at[1]),
        pltpu.make_async_copy(w_one, weights.at[0], local_sem.at[2]),
        pltpu.make_async_copy(w_two, weights.at[1], local_sem.at[3]),
    ]
    for load in loads:
        load.start()

    barrier = pltpu.get_barrier_semaphore()
    around = [(d, 0, 0) for d in STEP] + [(0, dy, dz) for dy, dz in PLANE]
    for d in around:

        @pl.when(has(*d))
        def _(d=d):
            pl.semaphore_signal(
                barrier, inc=1, device_id=(ix + d[0], iy + d[1], iz + d[2]), device_id_type=MESH
            )

    def remote(src, dst, index, d):
        return pltpu.make_async_remote_copy(
            src_ref=src,
            dst_ref=dst,
            send_sem=send_sem.at[index],
            recv_sem=recv_sem.at[index],
            device_id=(ix + d[0], iy + d[1], iz + d[2]),
            device_id_type=MESH,
        )

    def lanes_of(s):
        return pl.ds(0, 128) if s == 0 else pl.ds(384, 128)

    def x_copy(s, f):
        src = inputs[f].at[pl.ds(0, 2)] if s == 0 else inputs[f].at[pl.ds(2, 2)]
        dst = x_halo.at[f, pl.ds(2, 2)] if s == 0 else x_halo.at[f, pl.ds(0, 2)]
        d = (STEP[s], 0, 0)
        return remote(src, dst, X_MSG[s, f], d), has(*d), has(-d[0], 0, 0)

    def a_z_copy(s, f):
        d = (0, 0, STEP[s])
        src = inputs[f].at[:, :, lanes_of(s)]
        return remote(src, z_halo.at[0, s, f], A_Z[s, f], d), has(*d), has(0, 0, -d[2])

    def b_z_copy(s, k):
        d = (0, 0, STEP[s])
        src = x_halo.at[:, pl.ds(2 * k, 2), :, lanes_of(s)]
        dst = z_halo.at[1, s, :, pl.ds(2 * k, 2)]
        there = has(STEP[k], 0, 0)
        return remote(src, dst, B_Z[s, k], d), has(*d) & there, has(0, 0, -d[2]) & there

    def strip_copy(phase, s, z):
        d = (0, STEP[s], z - 1)
        src = strip_send.at[phase, s]
        if z == 0:
            src, dst = src.at[:, pl.ds(0, 128)], pl.ds(640, 128)
        elif z == 1:
            dst = pl.ds(128, 512)
        else:
            src, dst = src.at[:, pl.ds(384, 128)], pl.ds(0, 128)
        index = (A_S, B_S)[phase][s, z]
        return (
            remote(src, strip_halo.at[phase, s, :, dst], index, d),
            has(*d),
            has(0, -d[1], -d[2]),
        )

    x_copies = [x_copy(s, f) for s in range(2) for f in range(2)]
    a_copies = [a_z_copy(s, f) for s in range(2) for f in range(2)]
    a_strips = [strip_copy(0, s, z) for s in range(2) for z in range(3)]
    b_copies = [b_z_copy(s, k) for s in range(2) for k in range(2)]
    b_strips = [strip_copy(1, s, z) for s in range(2) for z in range(3)]

    def start(copies):
        for copy, send, _ in copies:
            pl.when(send)(copy.start)

    def wait_recv(copies):
        for copy, _, come in copies:
            pl.when(come)(copy.wait_recv)

    def wait_send(copies):
        for copy, send, _ in copies:
            pl.when(send)(copy.wait_send)

    arrivals = sum(has(*d).astype(jnp.int32) for d in around)
    pl.semaphore_wait(barrier, arrivals)
    start(x_copies)
    start(a_copies)

    loads[0].wait()
    loads[1].wait()
    pack_strips(own, strip_send.at[0])
    start(a_strips)

    for s in range(2):
        @pl.when(jnp.logical_not(has(STEP[s], 0, 0)))
        def _(s=s):
            x_halo[:, 2 * s : 2 * s + 2] = jnp.zeros((2, 2, 24, 512), BF16)
            for z in range(2):
                z_halo[1, z, :, 2 * s : 2 * s + 2] = jnp.zeros((2, 2, 24, 128), BF16)

        @pl.when(jnp.logical_not(has(0, 0, -STEP[s])))
        def _(s=s):
            z_halo[0, s] = jnp.zeros((2, 4, 24, 128), BF16)
            for k in range(2):

                @pl.when(has(STEP[k], 0, 0))
                def _():
                    z_halo[1, s, :, 2 * k : 2 * k + 2] = jnp.zeros((2, 2, 24, 128), BF16)

        for z, (lane, size) in enumerate(((640, 128), (128, 512), (0, 128))):

            @pl.when(jnp.logical_not(has(0, -STEP[s], 1 - z)))
            def _(s=s, lane=lane, size=size):
                for phase in range(2):
                    strip_halo[phase, s, :, lane : lane + size] = jnp.zeros((16, size), BF16)

    loads[2].wait()
    band_store(bands.at[0], weights.at[0])

    wait_recv(x_copies)
    pack_strips(x_halo, strip_send.at[1])
    start(b_copies)
    start(b_strips)

    loads[3].wait()
    band_store(bands.at[1], weights.at[1])

    wait_recv(a_copies)
    wait_recv(a_strips)
    assemble(grid, (2, 3, 4, 5), own, z_halo.at[0], strip_halo.at[0])

    bias_one = jnp.concatenate([b_one[...]] * 4, axis=1)
    bias_two = jnp.concatenate([b_two[...]] * 4, axis=1)

    def first_layer(begin, count):
        row = lax.broadcasted_iota(jnp.int32, (count, ROWS, 256), 1)
        lane = lax.broadcasted_iota(jnp.int32, (count, ROWS, 256), 2)
        layer = lax.broadcasted_iota(jnp.int32, (count, ROWS, 256), 0) + begin
        inside = (row < 24) | ((row == 24) & (iy < ny - 1)) | ((row == 31) & (iy > 0))
        inside &= (layer > 0) | (ix > 0)
        inside &= (layer < 5) | (ix < nx - 1)
        for block in range(3):
            size = 128 if block == 2 else 256
            conv = conv_narrow if block == 2 else conv_wide
            total = conv(grid, bands.at[0], begin, count, block * 256)
            value, slope = silu_pair(total, bias_one[:, :size])
            keep = inside[:, :, :size]
            if block == 0:
                keep &= (lane >= 64) | (iz > 0)
            if block == 2:
                keep &= (lane[:, :, :size] < 64) | (iz < nz - 1)
            for f, part in enumerate((value, slope)):
                hidden[f, begin : begin + count, :, block * 256 : block * 256 + size] = jnp.where(
                    keep, part, 0.0
                ).astype(BF16)

    first_layer(2, 2)

    wait_recv(b_copies)
    wait_recv(b_strips)
    assemble(grid, (0, 1, 6, 7), x_halo, z_halo.at[1], strip_halo.at[1])
    first_layer(0, 2)
    first_layer(4, 2)

    for block in range(2):
        total = conv_wide(hidden, bands.at[1], 0, 4, block * 256)
        value, slope = silu_pair(total, bias_two)
        cols = pl.ds(block * 256, 256)
        out[:, :, cols] = value[:, 0:24].astype(BF16)
        out_tangent[:, :, cols] = slope[:, 0:24].astype(BF16)

    wait_send(x_copies)
    wait_send(a_copies)
    wait_send(a_strips)
    wait_send(b_copies)
    wait_send(b_strips)


def solution(mesh):
    nx, ny, nz = mesh.shape["gx"], mesh.shape["gy"], mesh.shape["gz"]

    def shards(source, tangent, w_one, b_one, w_two, b_two):
        assert source.shape == (4, 24, 512)
        anywhere = pl.BlockSpec(memory_space=pl.ANY)
        vmem = pl.BlockSpec(memory_space=pltpu.VMEM)
        shape = jax.ShapeDtypeStruct(source.shape, source.dtype)
        return pl.pallas_call(
            functools.partial(kernel, nx, ny, nz),
            out_shape=(shape, shape),
            in_specs=[anywhere, anywhere, anywhere, vmem, anywhere, vmem],
            out_specs=(vmem, vmem),
            scratch_shapes=[
                pltpu.VMEM((2, 4, 24, 512), BF16),
                pltpu.VMEM((2, 4, 24, 512), BF16),
                pltpu.VMEM((2, 2, 2, 4, 24, 128), BF16),
                pltpu.VMEM((2, 2, 16, 512), BF16),
                pltpu.VMEM((2, 2, 16, 768), BF16),
                pltpu.VMEM((2, 3, 3, 3, 64, 64), BF16),
                pltpu.VMEM((2, 1152, 768), BF16),
                pltpu.VMEM((2, 8, ROWS, 768), BF16),
                pltpu.VMEM((2, 6, ROWS, 640), BF16),
                pltpu.SemaphoreType.DMA((4,)),
                pltpu.SemaphoreType.DMA((MESSAGES,)),
                pltpu.SemaphoreType.DMA((MESSAGES,)),
            ],
            compiler_params=pltpu.CompilerParams(
                collective_id=0, has_side_effects=True, vmem_limit_bytes=40 * 1024 * 1024
            ),
        )(source, tangent, w_one, b_one.reshape(1, 64), w_two, b_two.reshape(1, 64))

    return jax.shard_map(
        shards,
        mesh=mesh,
        in_specs=(P("gx", "gy", "gz"), P("gx", "gy", "gz"), P(), P(), P(), P()),
        out_specs=(P("gx", "gy", "gz"), P("gx", "gy", "gz")),
        check_vma=False,
    )
```

time: 74.1 us -> 21.7 us (0.29)
  starting transfers between devices: 24 us -> 0 us
  local copies, waits for them, and re-layouts: 23.7 us -> 5.75 us
  matrix products: 17 us -> 0 us
  Pallas kernels: 0 us -> 14.9 us
  waiting for transfers between devices: 4.17 us -> 0 us
  other arithmetic: 3.44 us -> 0 us
    ppermute x8 -> x0, starting transfers between devices: 24 us -> none  [the longest x4 17.3 us: padded_2(): lax.ppermute(tail, axis, [(i, (i + 1) % count) for i in range(ends)])]
    dot_general x56 -> x0, matrix products: 17 us -> none  [the longest x54 13.9 us: convolve(): jnp.einsum('sabcl,lm->sabcm', window, kernels[ox, oy, oz], preferred_elem...]
    convert_element_type x6 -> x0, local copies, waits for them, and re-layouts: 15.5 us -> none  [the longest x4 14.4 us: pair_kernels(): return mats.reshape(3, 3, 3, 2 * width, 2 * width).astype(jnp.bfloat16)]
    pallas_call x0 -> x1, Pallas kernels: none -> 14.9 us  [shards(): pl.pallas_call(functools.partial(kernel, nx, ny, nz), out_shape=(shape, s...]
    slice x8 -> x0, local copies, waits for them, and re-layouts: 6.16 us -> none  [the longest x4 5.35 us: convolve(): window = view[:, ox:ox + out_x, oy:oy + out_y, oz:oz + pairs, :]]
    unnamed x13 -> x14, local copies, waits for them, and re-layouts: 0.05 us -> 5.75 us
    ppermute x8 -> x0, waiting for transfers between devices: 4.17 us -> none  [the longest x4 4.16 us: padded_2(): lax.ppermute(head, axis, [((i + 1) % count, i) for i in range(ends)])]
    convert_element_type x3 -> x0, other arithmetic: 1.74 us -> none  [the longest x1 0.9 us: shards(): (silu_slope(pre_one) * first[1] * inside).astype(jnp.bfloat16)]
  transfers between devices with their start and end apart: 8 -> 0, of which waited for: 2 -> 0; matrix products, arithmetic and copies ran while one was open for 24% -> 0% of each run, Pallas kernels for 0% -> 0%
where the time goes in v1:
time: 21.7 us; the launch traced here: 21.3 us
  Pallas kernels  14.9 us (69%)
  local copies, waits for them, and re-layouts  5.75 us (26%)
  between operations  0.66 us (3%)
    pallas_call x1, Pallas kernels, shards(): pl.pallas_call(functools.partial(kernel, nx, ny, nz), out_shape=(shape, s...  14.9 us
    unnamed x14, local copies, waits for them, and re-layouts  5.75 us

profile of v1, /device:TPU:1, one launch (start us, length us, event | category | flops | bytes accessed | tf_op | source)
XLA Modules:
  0.0 21.3 jit_solution(9739365643630582711)
XLA Ops:
  0.6 0.0 copy-start.4
  0.6 0.0 copy-start.5
  0.7 0.6 %copy-done.4 = f32[64]{0:T(128)S(1)} copy-done((f32[64]{0:T(128)S(1)}, f32[64]{0:T(128)}, u32[]{:S(2)}) %copy-start.4) | copy-done | bytes 280
  1.3 0.0 copy-done.5
  1.3 0.0 copy-start
  1.3 1.0 %copy-done = bf16[3,3,3,64,64]{4,3,2,1,0:T(8,128)(2,1)S(1)} copy-done((bf16[3,3,3,64,64]{4,3,2,1,0:T(8,128)(2,1)S(1)}, bf16[3,3,3,64,64]{4,3,2,1,0:T(8,128)(2,1)}, u32[]{:S(2)}) %copy-start) | copy-done | bytes 221208
  2.3 0.0 copy-start.1
  2.3 1.0 %copy-done.1 = bf16[3,3,3,64,64]{4,3,2,1,0:T(8,128)(2,1)S(1)} copy-done((bf16[3,3,3,64,64]{4,3,2,1,0:T(8,128)(2,1)S(1)}, bf16[3,3,3,64,64]{4,3,2,1,0:T(8,128)(2,1)}, u32[]{:S(2)}) %copy-start.1) | copy-done | bytes 221208
  3.3 0.0 copy-start.2
  3.3 0.9 %copy-done.2 = bf16[4,24,512]{2,1,0:T(8,128)(2,1)S(1)} copy-done((bf16[4,24,512]{2,1,0:T(8,128)(2,1)S(1)}, bf16[4,24,512]{2,1,0:T(8,128)(2,1)}, u32[]{:S(2)}) %copy-start.2) | copy-done | bytes 98328
  4.2 0.0 copy-start.3
  4.2 0.9 %copy-done.3 = bf16[4,24,512]{2,1,0:T(8,128)(2,1)S(1)} copy-done((bf16[4,24,512]{2,1,0:T(8,128)(2,1)S(1)}, bf16[4,24,512]{2,1,0:T(8,128)(2,1)}, u32[]{:S(2)}) %copy-start.3) | copy-done | bytes 98328
  5.1 14.9 %shard_map.77 = (bf16[4,24,512]{2,1,0:T(8,128)(2,1)S(1)}, bf16[4,24,512]{2,1,0:T(8,128)(2,1)S(1)}) custom-call(bf16[4,24,512]{2,1,0:T(8,128)(2,1)S(1)} %copy-done.2, bf16[4,24,512]{2,1,0:T(8,128)(2,1)S(1)} %copy-done.3, bf16[3,3,3,64,64]{4,3,2,1,0:T(8,128)(2,1)S(1)} %copy-done, f32[1,64]{1,0:T(1,128)S(1)} %bitcast.2, ...), custom_call_target="tpu_custom_call" | custom-call | tf_op jit(solution)/shard_map/pallas_call | solution.py:354
  20.0 0.6 %copy.10 = bf16[4,24,512]{2,1,0:T(8,128)(2,1)} copy(bf16[4,24,512]{2,1,0:T(8,128)(2,1)S(1)} %get-tuple-element.4) | data formatting | bytes 196608
  20.7 0.6 %copy.11 = bf16[4,24,512]{2,1,0:T(8,128)(2,1)} copy(bf16[4,24,512]{2,1,0:T(8,128)(2,1)S(1)} %get-tuple-element.5) | data formatting | bytes 196608
Async XLA Ops:
  0.6 0.7 %copy-start.4 = (f32[64]{0:T(128)S(1)}, f32[64]{0:T(128)}, u32[]{:S(2)}) copy-start(f32[64]{0:T(128)} %param.9) | copy-start | bytes 772
  0.6 0.7 %copy-start.5 = (f32[64]{0:T(128)S(1)}, f32[64]{0:T(128)}, u32[]{:S(2)}) copy-start(f32[64]{0:T(128)} %param.11) | copy-start | bytes 772
  1.3 1.0 %copy-start = (bf16[3,3,3,64,64]{4,3,2,1,0:T(8,128)(2,1)S(1)}, bf16[3,3,3,64,64]{4,3,2,1,0:T(8,128)(2,1)}, u32[]{:S(2)}) copy-start(bf16[3,3,3,64,64]{4,3,2,1,0:T(8,128)(2,1)} %w_one.1) | copy-start | bytes 663556
  2.3 1.0 %copy-start.1 = (bf16[3,3,3,64,64]{4,3,2,1,0:T(8,128)(2,1)S(1)}, bf16[3,3,3,64,64]{4,3,2,1,0:T(8,128)(2,1)}, u32[]{:S(2)}) copy-start(bf16[3,3,3,64,64]{4,3,2,1,0:T(8,128)(2,1)} %w_two.1) | copy-start | bytes 663556
  3.3 0.9 %copy-start.2 = (bf16[4,24,512]{2,1,0:T(8,128)(2,1)S(1)}, bf16[4,24,512]{2,1,0:T(8,128)(2,1)}, u32[]{:S(2)}) copy-start(bf16[4,24,512]{2,1,0:T(8,128)(2,1)} %source.1) | copy-start | bytes 294916
  4.2 0.9 %copy-start.3 = (bf16[4,24,512]{2,1,0:T(8,128)(2,1)S(1)}, bf16[4,24,512]{2,1,0:T(8,128)(2,1)}, u32[]{:S(2)}) copy-start(bf16[4,24,512]{2,1,0:T(8,128)(2,1)} %tangent.1) | copy-start | bytes 294916

commit v2 on v1

--- a/solution.py
+++ b/solution.py
@@ -11,13 +11,9 @@
 F32 = jnp.float32
 BF16 = jnp.bfloat16
 ROWS = 32
-PLANE = [(dy, dz) for dy in (-1, 0, 1) for dz in (-1, 0, 1) if dy or dz]
-X_MSG = {(s, f): 2 * s + f for s in range(2) for f in range(2)}
-A_Z = {(s, f): 4 + 2 * s + f for s in range(2) for f in range(2)}
-A_S = {(s, z): 8 + 3 * s + z for s in range(2) for z in range(3)}
-B_Z = {(s, k): 14 + 2 * s + k for s in range(2) for k in range(2)}
-B_S = {(s, z): 18 + 3 * s + z for s in range(2) for z in range(3)}
-MESSAGES = 24
+AROUND = [
+    (dx, dy, dz) for dx in (-1, 0, 1) for dy in (-1, 0, 1) for dz in (-1, 0, 1) if dx or dy or dz
+]
 STEP = (-1, 1)
 
 
@@ -63,18 +59,19 @@
     strips[1] = jnp.concatenate(high, axis=0).astype(BF16)
 
 
-def assemble(grid, places, field, z_halo, strips):
+def assemble(grid, places, field, z_halo, strips, packed):
     row = lax.broadcasted_iota(jnp.int32, (8, 768), 0)
     for f in range(2):
-        above = strips[1].astype(F32)[8 * f : 8 * f + 8]
-        below = strips[0].astype(F32)[8 * f : 8 * f + 8]
         for x in range(4):
             place = places[x]
             grid[f, place, 0:24, 0:128] = z_halo[1, f, x]
             grid[f, place, 0:24, 128:640] = field[f, x]
             grid[f, place, 0:24, 640:768] = z_halo[0, f, x]
-            down = pltpu.roll(below, (8 - 2 * x) % 8, 0) if x else below
-            up = pltpu.roll(above, 6 - 2 * x, 0) if x != 3 else above
+            at = packed[x]
+            down = strips[x][0].astype(F32)[8 * f : 8 * f + 8]
+            up = strips[x][1].astype(F32)[8 * f : 8 * f + 8]
+            down = pltpu.roll(down, 8 - 2 * at, 0) if at else down
+            up = pltpu.roll(up, 6 - 2 * at, 0) if at != 3 else up
             edge = jnp.where(row < 2, down, jnp.where(row >= 6, up, 0.0))
             grid[f, place, 24:32, :] = edge.astype(BF16)
 
@@ -146,6 +143,7 @@
     strip_send,
     strip_halo,
     weights,
+    biases,
     bands,
     grid,
     hidden,
@@ -163,19 +161,19 @@
                 ok = this if ok is None else ok & this
         return ok
 
-    inputs = (source, tangent)
     loads = [
         pltpu.make_async_copy(source, own.at[0], local_sem.at[0]),
         pltpu.make_async_copy(tangent, own.at[1], local_sem.at[1]),
         pltpu.make_async_copy(w_one, weights.at[0], local_sem.at[2]),
         pltpu.make_async_copy(w_two, weights.at[1], local_sem.at[3]),
+        pltpu.make_async_copy(b_one, biases.at[0], local_sem.at[4]),
+        pltpu.make_async_copy(b_two, biases.at[1], local_sem.at[5]),
     ]
     for load in loads:
         load.start()
 
     barrier = pltpu.get_barrier_semaphore()
-    around = [(d, 0, 0) for d in STEP] + [(0, dy, dz) for dy, dz in PLANE]
-    for d in around:
+    for d in AROUND:
 
         @pl.when(has(*d))
         def _(d=d):
@@ -196,45 +194,31 @@
     def lanes_of(s):
         return pl.ds(0, 128) if s == 0 else pl.ds(384, 128)
 
-    def x_copy(s, f):
-        src = inputs[f].at[pl.ds(0, 2)] if s == 0 else inputs[f].at[pl.ds(2, 2)]
-        dst = x_halo.at[f, pl.ds(2, 2)] if s == 0 else x_halo.at[f, pl.ds(0, 2)]
-        d = (STEP[s], 0, 0)
-        return remote(src, dst, X_MSG[s, f], d), has(*d), has(-d[0], 0, 0)
-
-    def a_z_copy(s, f):
-        d = (0, 0, STEP[s])
-        src = inputs[f].at[:, :, lanes_of(s)]
-        return remote(src, z_halo.at[0, s, f], A_Z[s, f], d), has(*d), has(0, 0, -d[2])
-
-    def b_z_copy(s, k):
-        d = (0, 0, STEP[s])
-        src = x_halo.at[:, pl.ds(2 * k, 2), :, lanes_of(s)]
-        dst = z_halo.at[1, s, :, pl.ds(2 * k, 2)]
-        there = has(STEP[k], 0, 0)
-        return remote(src, dst, B_Z[s, k], d), has(*d) & there, has(0, 0, -d[2]) & there
-
-    def strip_copy(phase, s, z):
-        d = (0, STEP[s], z - 1)
-        src = strip_send.at[phase, s]
-        if z == 0:
-            src, dst = src.at[:, pl.ds(0, 128)], pl.ds(640, 128)
-        elif z == 1:
-            dst = pl.ds(128, 512)
+    def copy_to(d):
+        dx, dy, dz = d
+        if dy == 0:
+            slot = pl.ds(0, 4) if dx == 0 else pl.ds(0 if dx > 0 else 2, 2)
+            layers = pl.ds(0, 4) if dx == 0 else pl.ds(2 if dx > 0 else 0, 2)
+            if dz == 0:
+                src, dst = own.at[:, layers], x_halo.at[:, slot]
+            else:
+                src = own.at[:, layers, :, lanes_of(dz > 0)]
+                dst = z_halo.at[int(dx != 0), int(dz > 0), :, slot]
         else:
-            src, dst = src.at[:, pl.ds(384, 128)], pl.ds(0, 128)
-        index = (A_S, B_S)[phase][s, z]
-        return (
-            remote(src, strip_halo.at[phase, s, :, dst], index, d),
-            has(*d),
-            has(0, -d[1], -d[2]),
-        )
-
-    x_copies = [x_copy(s, f) for s in range(2) for f in range(2)]
-    a_copies = [a_z_copy(s, f) for s in range(2) for f in range(2)]
-    a_strips = [strip_copy(0, s, z) for s in range(2) for z in range(3)]
-    b_copies = [b_z_copy(s, k) for s in range(2) for k in range(2)]
-    b_strips = [strip_copy(1, s, z) for s in range(2) for z in range(3)]
+            src = strip_send.at[int(dy > 0)]
+            if dz == 0:
+                dst = pl.ds(128, 512)
+            else:
+                src = src.at[:, lanes_of(dz > 0)]
+                dst = pl.ds(0 if dz > 0 else 640, 128)
+            dst = strip_halo.at[dx + 1, int(dy > 0), :, dst]
+        return remote(src, dst, AROUND.index(d), d), has(*d), has(-dx, -dy, -dz)
+
+    def group(depth, strip):
+        return [copy_to(d) for d in AROUND if (d[0] != 0) == depth and (d[1] != 0) == strip]
+
+    x_copies, x_strips = group(True, False), group(True, True)
+    a_copies, a_strips = group(False, False), group(False, True)
 
     def start(copies):
         for copy, send, _ in copies:
@@ -248,14 +232,15 @@
         for copy, send, _ in copies:
             pl.when(send)(copy.wait_send)
 
-    arrivals = sum(has(*d).astype(jnp.int32) for d in around)
+    arrivals = sum(has(*d).astype(jnp.int32) for d in AROUND)
     pl.semaphore_wait(barrier, arrivals)
+    loads[0].wait()
+    loads[1].wait()
     start(x_copies)
     start(a_copies)
 
-    loads[0].wait()
-    loads[1].wait()
-    pack_strips(own, strip_send.at[0])
+    pack_strips(own, strip_send)
+    start(x_strips)
     start(a_strips)
 
     for s in range(2):
@@ -264,6 +249,7 @@
             x_halo[:, 2 * s : 2 * s + 2] = jnp.zeros((2, 2, 24, 512), BF16)
             for z in range(2):
                 z_halo[1, z, :, 2 * s : 2 * s + 2] = jnp.zeros((2, 2, 24, 128), BF16)
+                strip_halo[2 - 2 * s, z] = jnp.zeros((16, 768), BF16)
 
         @pl.when(jnp.logical_not(has(0, 0, -STEP[s])))
         def _(s=s):
@@ -278,26 +264,23 @@
 
             @pl.when(jnp.logical_not(has(0, -STEP[s], 1 - z)))
             def _(s=s, lane=lane, size=size):
-                for phase in range(2):
-                    strip_halo[phase, s, :, lane : lane + size] = jnp.zeros((16, size), BF16)
+                for side in range(3):
+                    strip_halo[side, s, :, lane : lane + size] = jnp.zeros((16, size), BF16)
 
     loads[2].wait()
     band_store(bands.at[0], weights.at[0])
 
-    wait_recv(x_copies)
-    pack_strips(x_halo, strip_send.at[1])
-    start(b_copies)
-    start(b_strips)
-
     loads[3].wait()
     band_store(bands.at[1], weights.at[1])
 
     wait_recv(a_copies)
     wait_recv(a_strips)
-    assemble(grid, (2, 3, 4, 5), own, z_halo.at[0], strip_halo.at[0])
-
-    bias_one = jnp.concatenate([b_one[...]] * 4, axis=1)
-    bias_two = jnp.concatenate([b_two[...]] * 4, axis=1)
+    assemble(grid, (2, 3, 4, 5), own, z_halo.at[0], (strip_halo.at[1],) * 4, range(4))
+
+    loads[4].wait()
+    loads[5].wait()
+    bias_one = jnp.concatenate([biases[0]] * 4, axis=1)
+    bias_two = jnp.concatenate([biases[1]] * 4, axis=1)
 
     def first_layer(begin, count):
         row = lax.broadcasted_iota(jnp.int32, (count, ROWS, 256), 1)
@@ -323,9 +306,9 @@
 
     first_layer(2, 2)
 
-    wait_recv(b_copies)
-    wait_recv(b_strips)
-    assemble(grid, (0, 1, 6, 7), x_halo, z_halo.at[1], strip_halo.at[1])
+    wait_recv(x_copies)
+    wait_recv(x_strips)
+    assemble(grid, (0, 1, 6, 7), x_halo, z_halo.at[1], (strip_halo.at[2],) * 2 + (strip_halo.at[0],) * 2, (2, 3, 0, 1))
     first_layer(0, 2)
     first_layer(4, 2)
 
@@ -339,8 +322,7 @@
     wait_send(x_copies)
     wait_send(a_copies)
     wait_send(a_strips)
-    wait_send(b_copies)
-    wait_send(b_strips)
+    wait_send(x_strips)
 
 
 def solution(mesh):
@@ -348,33 +330,33 @@
 
     def shards(source, tangent, w_one, b_one, w_two, b_two):
         assert source.shape == (4, 24, 512)
-        anywhere = pl.BlockSpec(memory_space=pl.ANY)
+        hbm = pl.BlockSpec(memory_space=pltpu.HBM)
         vmem = pl.BlockSpec(memory_space=pltpu.VMEM)
         shape = jax.ShapeDtypeStruct(source.shape, source.dtype)
         return pl.pallas_call(
             functools.partial(kernel, nx, ny, nz),
             out_shape=(shape, shape),
-            in_specs=[anywhere, anywhere, anywhere, vmem, anywhere, vmem],
+            in_specs=[hbm] * 6,
             out_specs=(vmem, vmem),
             scratch_shapes=[
                 pltpu.VMEM((2, 4, 24, 512), BF16),
                 pltpu.VMEM((2, 4, 24, 512), BF16),
                 pltpu.VMEM((2, 2, 2, 4, 24, 128), BF16),
-                pltpu.VMEM((2, 2, 16, 512), BF16),
-                pltpu.VMEM((2, 2, 16, 768), BF16),
+                pltpu.VMEM((2, 16, 512), BF16),
+                pltpu.VMEM((3, 2, 16, 768), BF16),
                 pltpu.VMEM((2, 3, 3, 3, 64, 64), BF16),
+                pltpu.VMEM((2, 1, 64), F32),
                 pltpu.VMEM((2, 1152, 768), BF16),
                 pltpu.VMEM((2, 8, ROWS, 768), BF16),
                 pltpu.VMEM((2, 6, ROWS, 640), BF16),
-                pltpu.SemaphoreType.DMA((4,)),
-                pltpu.SemaphoreType.DMA((MESSAGES,)),
-                pltpu.SemaphoreType.DMA((MESSAGES,)),
+                pltpu.SemaphoreType.DMA((6,)),
+                pltpu.SemaphoreType.DMA((len(AROUND),)),
+                pltpu.SemaphoreType.DMA((len(AROUND),)),
             ],
             compiler_params=pltpu.CompilerParams(
-                collective_id=0, has_side_effects=True, vmem_limit_bytes=40 * 1024 * 1024
+                collective_id=0, has_side_effects=True, vmem_limit_bytes=64 * 1024 * 1024
             ),
         )(source, tangent, w_one, b_one.reshape(1, 64), w_two, b_two.reshape(1, 64))
-
     return jax.shard_map(
         shards,
         mesh=mesh,

time: 21.7 us -> 15.7 us (0.72)
  local copies, waits for them, and re-layouts: 5.75 us -> 2.22 us
  Pallas kernels: 14.9 us -> 12.6 us
    unnamed x14 -> x4, local copies, waits for them, and re-layouts: 5.75 us -> 2.22 us
    pallas_call x1, Pallas kernels: 14.9 us -> 12.6 us  [shards(): pl.pallas_call(functools.partial(kernel, nx, ny, nz), out_shape=(shape, s...]
where the time goes in v2:
time: 15.7 us; the launch traced here: 15.5 us
  Pallas kernels  12.6 us (80%)
  local copies, waits for them, and re-layouts  2.22 us (14%)
  between operations  0.65 us (4%)
    pallas_call x1, Pallas kernels, shards(): pl.pallas_call(functools.partial(kernel, nx, ny, nz), out_shape=(shape, s...  12.6 us
    unnamed x4, local copies, waits for them, and re-layouts  2.22 us

profile of v2, /device:TPU:1, one launch (start us, length us, event | category | flops | bytes accessed | tf_op | source)
XLA Modules:
  0.0 15.5 jit_solution(10822575627159909588)
XLA Ops:
  0.6 12.6 %shard_map.77 = (bf16[4,24,512]{2,1,0:T(8,128)(2,1)}, bf16[4,24,512]{2,1,0:T(8,128)(2,1)}) custom-call(bf16[4,24,512]{2,1,0:T(8,128)(2,1)} %source.1, bf16[4,24,512]{2,1,0:T(8,128)(2,1)} %tangent.1, bf16[3,3,3,64,64]{4,3,2,1,0:T(8,128)(2,1)} %w_one.1, f32[1,64]{1,0:T(1,128)} %bitcast.2, bf16[3,3,3,64,64]{4,3,2,1,0:T(8,128)(2,1)} %w_two.1, f32[1,64]{1,0:T(1,128)} %bitcast.3), custom_call_target="tpu_custom_call" | custom-call | tf_op jit(solution)/shard_map/pallas_call | solution.py:336
  13.3 0.0 copy-start
  13.3 1.6 %copy.10 = bf16[4,24,512]{2,1,0:T(8,128)(2,1)} copy(bf16[4,24,512]{2,1,0:T(8,128)(2,1)} %get-tuple-element.4) | data formatting | bytes 196608
  14.9 0.0 copy-done
  14.9 0.6 %copy.11 = bf16[4,24,512]{2,1,0:T(8,128)(2,1)} copy(bf16[4,24,512]{2,1,0:T(8,128)(2,1)S(1)} %copy-done) | data formatting | bytes 196608
Async XLA Ops:
  13.3 1.6 %copy-start = (bf16[4,24,512]{2,1,0:T(8,128)(2,1)S(1)}, bf16[4,24,512]{2,1,0:T(8,128)(2,1)}, u32[]{:S(2)}) copy-start(bf16[4,24,512]{2,1,0:T(8,128)(2,1)} %get-tuple-element.5) | copy-start | bytes 294916

commit v3 on v2

--- a/solution.py
+++ b/solution.py
@@ -332,7 +332,7 @@
         assert source.shape == (4, 24, 512)
         hbm = pl.BlockSpec(memory_space=pltpu.HBM)
         vmem = pl.BlockSpec(memory_space=pltpu.VMEM)
-        shape = jax.ShapeDtypeStruct(source.shape, source.dtype)
+        shape = pltpu.VMEM(source.shape, source.dtype)
         return pl.pallas_call(
             functools.partial(kernel, nx, ny, nz),
             out_shape=(shape, shape),
@@ -354,7 +354,7 @@
                 pltpu.SemaphoreType.DMA((len(AROUND),)),
             ],
             compiler_params=pltpu.CompilerParams(
-                collective_id=0, has_side_effects=True, vmem_limit_bytes=64 * 1024 * 1024
+                collective_id=0, has_side_effects=True, vmem_limit_bytes=62 * 1024 * 1024
             ),
         )(source, tangent, w_one, b_one.reshape(1, 64), w_two, b_two.reshape(1, 64))
     return jax.shard_map(

time: 15.7 us -> 14 us (0.89)
  local copies, waits for them, and re-layouts: 2.22 us -> 1.28 us
  Pallas kernels: 12.6 us -> 12 us
    unnamed x4 -> x2, local copies, waits for them, and re-layouts: 2.22 us -> 1.28 us
    pallas_call x1, Pallas kernels: 12.6 us -> 12 us  [shards(): pl.pallas_call(functools.partial(kernel, nx, ny, nz), out_shape=(shape, s...]
where the time goes in v3:
time: 14 us; the launch traced here: 13.9 us
  Pallas kernels  12 us (86%)
  local copies, waits for them, and re-layouts  1.28 us (9%)
  between operations  0.64 us (5%)
    pallas_call x1, Pallas kernels, shards(): pl.pallas_call(functools.partial(kernel, nx, ny, nz), out_shape=(shape, s...  12 us
    unnamed x2, local copies, waits for them, and re-layouts  1.28 us

profile of v3, /device:TPU:1, one launch (start us, length us, event | category | flops | bytes accessed | tf_op | source)
XLA Modules:
  0.0 13.9 jit_solution(17551677595086062872)
XLA Ops:
  0.6 12.0 %shard_map.77 = (bf16[4,24,512]{2,1,0:T(8,128)(2,1)S(1)}, bf16[4,24,512]{2,1,0:T(8,128)(2,1)S(1)}) custom-call(bf16[4,24,512]{2,1,0:T(8,128)(2,1)} %source.1, bf16[4,24,512]{2,1,0:T(8,128)(2,1)} %tangent.1, bf16[3,3,3,64,64]{4,3,2,1,0:T(8,128)(2,1)} %w_one.1, f32[1,64]{1,0:T(1,128)} %bitcast.2, bf16[3,3,3,64,64]{4,3,2,1,0:T(8,128)(2,1)} %w_two.1, ...), custom_call_target="tpu_custom_call" | custom-call | tf_op jit(solution)/shard_map/pallas_call | solution.py:336
  12.6 0.6 %copy.10 = bf16[4,24,512]{2,1,0:T(8,128)(2,1)} copy(bf16[4,24,512]{2,1,0:T(8,128)(2,1)S(1)} %get-tuple-element.2) | data formatting | bytes 196608
  13.3 0.6 %copy.11 = bf16[4,24,512]{2,1,0:T(8,128)(2,1)} copy(bf16[4,24,512]{2,1,0:T(8,128)(2,1)S(1)} %get-tuple-element.3) | data formatting | bytes 196608

commit v4 on v3

--- a/solution.py
+++ b/solution.py
@@ -314,10 +314,9 @@
 
     for block in range(2):
         total = conv_wide(hidden, bands.at[1], 0, 4, block * 256)
-        value, slope = silu_pair(total, bias_two)
         cols = pl.ds(block * 256, 256)
-        out[:, :, cols] = value[:, 0:24].astype(BF16)
-        out_tangent[:, :, cols] = slope[:, 0:24].astype(BF16)
+        out[:, :, cols] = total[0, :, 0:24] + bias_two
+        out_tangent[:, :, cols] = total[1, :, 0:24]
 
     wait_send(x_copies)
     wait_send(a_copies)
@@ -332,8 +331,8 @@
         assert source.shape == (4, 24, 512)
         hbm = pl.BlockSpec(memory_space=pltpu.HBM)
         vmem = pl.BlockSpec(memory_space=pltpu.VMEM)
-        shape = pltpu.VMEM(source.shape, source.dtype)
-        return pl.pallas_call(
+        shape = pltpu.VMEM(source.shape, F32)
+        pre, direction = pl.pallas_call(
             functools.partial(kernel, nx, ny, nz),
             out_shape=(shape, shape),
             in_specs=[hbm] * 6,
@@ -357,6 +356,8 @@
                 collective_id=0, has_side_effects=True, vmem_limit_bytes=62 * 1024 * 1024
             ),
         )(source, tangent, w_one, b_one.reshape(1, 64), w_two, b_two.reshape(1, 64))
+        sig = jax.nn.sigmoid(pre)
+        return (pre * sig).astype(BF16), (sig * (1.0 + pre * (1.0 - sig)) * direction).astype(BF16)
     return jax.shard_map(
         shards,
         mesh=mesh,

time: 14 us -> 13.5 us (0.964)
  local copies, waits for them, and re-layouts: 1.28 us -> 0 us
  other arithmetic: 0 us -> 0.76 us
    unnamed x2 -> x0, local copies, waits for them, and re-layouts: 1.28 us -> none
    convert_element_type x0 -> x1, other arithmetic: none -> 0.76 us  [shards(): (sig * (1.0 + pre * (1.0 - sig)) * direction).astype(BF16)]
where the time goes in v4:
time: 13.5 us; the launch traced here: 13.4 us
  Pallas kernels  12 us (89%)
  other arithmetic  0.76 us (6%)
  between operations  0.64 us (5%)
    pallas_call x1, Pallas kernels, shards(): pl.pallas_call(functools.partial(kernel, nx, ny, nz), out_shape=(shape, s...  12 us
    convert_element_type x1, other arithmetic, shards(): (sig * (1.0 + pre * (1.0 - sig)) * direction).astype(BF16)  0.76 us

profile of v4, /device:TPU:1, one launch (start us, length us, event | category | flops | bytes accessed | tf_op | source)
XLA Modules:
  0.0 13.4 jit_solution(15615748101975132302)
XLA Ops:
  0.6 12.0 %shard_map.77 = (f32[4,24,512]{2,1,0:T(8,128)S(1)}, f32[4,24,512]{2,1,0:T(8,128)S(1)}) custom-call(bf16[4,24,512]{2,1,0:T(8,128)(2,1)} %source.1, bf16[4,24,512]{2,1,0:T(8,128)(2,1)} %tangent.1, bf16[3,3,3,64,64]{4,3,2,1,0:T(8,128)(2,1)} %w_one.1, f32[1,64]{1,0:T(1,128)} %bitcast.2, bf16[3,3,3,64,64]{4,3,2,1,0:T(8,128)(2,1)} %w_two.1, f32[1,64]{1,0:T(1,128)} %bitcast.3), custom_call_target="tpu_custom_call" | custom-call | tf_op jit(solution)/shard_map/pallas_call | solution.py:335
  12.6 0.8 %multiply_convert_fusion = (bf16[4,24,512]{2,1,0:T(8,128)(2,1)}, bf16[4,24,512]{2,1,0:T(8,128)(2,1)}) fusion(f32[4,24,512]{2,1,0:T(8,128)S(1)} %get-tuple-element.5, f32[4,24,512]{2,1,0:T(8,128)S(1)} %get-tuple-element.4), kind=kLoop, calls=%fused_computation | loop fusion | flops 540672 | bytes 589824 | tf_op jit(solution)/shard_map/convert_element_type | solution.py:360

commit v5 on v4

--- a/solution.py
+++ b/solution.py
@@ -240,8 +240,8 @@
     start(a_copies)
 
     pack_strips(own, strip_send)
+    start(a_strips)
     start(x_strips)
-    start(a_strips)
 
     for s in range(2):
         @pl.when(jnp.logical_not(has(STEP[s], 0, 0)))

time: 13.5 us -> 13.5 us (level)
  no operation moved by 1% of the time
where the time goes in v5:
time: 13.5 us; the launch traced here: 13.4 us
  Pallas kernels  12 us (89%)
  other arithmetic  0.76 us (6%)
  between operations  0.64 us (5%)
    pallas_call x1, Pallas kernels, shards(): pl.pallas_call(functools.partial(kernel, nx, ny, nz), out_shape=(shape, s...  12 us
    convert_element_type x1, other arithmetic, shards(): (sig * (1.0 + pre * (1.0 - sig)) * direction).astype(BF16)  0.76 us

profile of v5, /device:TPU:1, one launch (start us, length us, event | category | flops | bytes accessed | tf_op | source)
XLA Modules:
  0.0 13.4 jit_solution(11127942087282955130)
XLA Ops:
  0.6 12.0 %shard_map.77 = (f32[4,24,512]{2,1,0:T(8,128)S(1)}, f32[4,24,512]{2,1,0:T(8,128)S(1)}) custom-call(bf16[4,24,512]{2,1,0:T(8,128)(2,1)} %source.1, bf16[4,24,512]{2,1,0:T(8,128)(2,1)} %tangent.1, bf16[3,3,3,64,64]{4,3,2,1,0:T(8,128)(2,1)} %w_one.1, f32[1,64]{1,0:T(1,128)} %bitcast.2, bf16[3,3,3,64,64]{4,3,2,1,0:T(8,128)(2,1)} %w_two.1, f32[1,64]{1,0:T(1,128)} %bitcast.3), custom_call_target="tpu_custom_call" | custom-call | tf_op jit(solution)/shard_map/pallas_call | solution.py:335
  12.6 0.8 %multiply_convert_fusion = (bf16[4,24,512]{2,1,0:T(8,128)(2,1)}, bf16[4,24,512]{2,1,0:T(8,128)(2,1)}) fusion(f32[4,24,512]{2,1,0:T(8,128)S(1)} %get-tuple-element.5, f32[4,24,512]{2,1,0:T(8,128)S(1)} %get-tuple-element.4), kind=kLoop, calls=%fused_computation | loop fusion | flops 540672 | bytes 589824 | tf_op jit(solution)/shard_map/convert_element_type | solution.py:360
